TPU v7x, 128 devices: a whole 4x4x4 slice. The times are simulated.
128 devices in a mesh: attn: 8 (over z, core), expert: 16 (over x, y).
Axes of the slice: x: 4, y: 4, z: 4, core: 2. Of those that a mesh axis runs over, the one named last changes fastest.
Arguments:
- queries: bfloat16 [32, 64, 576], P('attn'), may hold values from -11 to 11
- cache: bfloat16 [24576, 64, 576], P(('attn', 'expert')), may hold values from -6 to 6
- owner: int32 [24576], P(('attn', 'expert')), may hold values from 0 to 4, as said below
- uv_weight: bfloat16 [64, 512, 128], P('expert'), may hold values from -0.25 to 0.25
- out_weight: bfloat16 [8192, 7168], P('expert')
- norm_gain: float32 [7168], replicated, may hold values from 0.1 to 1.9
- expert_ids: int32 [32, 8], P('attn'), may hold values from 0 to 15, all different within a row; in each aligned block of 4 rows (0 to 3, 4 to 7, ...) at most 4 rows name the same one
- gate_values: float32 [32, 8], P('attn'), may hold values from 0.1 to 1
- gate_weight: bfloat16 [16, 7168, 2048], P('attn', None, 'expert'), may hold values from -0.0625 to 0.0625
- up_weight: bfloat16 [16, 7168, 2048], P('attn', None, 'expert'), may hold values from -0.0625 to 0.0625
- down_weight: bfloat16 [16, 2048, 7168], P('attn', 'expert'), may hold values from -0.1875 to 0.1875
Outputs:
- layer_out: bfloat16 [32, 7168], P('attn', 'expert')
Inputs may be any that keep to these rules, and one draw needn't show every extreme that they name: owner[p] names one of the 4 requests of page p's attention index, or is 4 for an empty slot; every request holds at least one page. `expert_ids`: among the rows of one attention index, no expert is named by more than 4 rows.
All inputs are finite; a program needn't handle non-finite values.
Results may differ from a plain program's by a relative error of at most 0.035.
Values may be sent and summed in bfloat16 or wider, within the bound.
A program may use at most 192 MiB of HBM per device.

v0:
```python
import jax
import jax.numpy as jnp
from jax import lax
from jax.sharding import PartitionSpec as P

NEGATIVE = -1e30
SCORE_SCALE = 192.0 ** (-0.5)
EPSILON = 1e-06
HIGHEST = lax.Precision.HIGHEST


def local_attention(queries, cache, owner, latent_width):
    row_count = queries.shape[0]
    head_count = queries.shape[1]
    pool_size = cache.shape[0]
    valid_pages = owner < row_count
    safe_owner = jnp.minimum(owner, row_count - 1)
    picked = jnp.take(queries, safe_owner, axis=0)
    scores = (
        jnp.einsum("phc,ptc->pht", picked, cache, preferred_element_type=jnp.float32) * SCORE_SCALE
    )
    page_max = jnp.where(valid_pages[:, None], jnp.max(scores, axis=2), NEGATIVE)
    member = (safe_owner[:, None] == jnp.arange(row_count, dtype=jnp.int32)[None, :]) & valid_pages[
        :, None
    ]
    row_max = jnp.max(jnp.where(member[:, :, None], page_max[:, None, :], NEGATIVE), axis=0)
    weights = jnp.where(
        valid_pages[:, None, None],
        jnp.exp(scores - jnp.take(row_max, safe_owner, axis=0)[:, :, None]),
        0.0,
    )
    probs = weights.astype(jnp.bfloat16)
    page_sum = jnp.einsum(
        "pht,ptc->phc", probs, cache[:, :, :latent_width], preferred_element_type=jnp.float32
    )
    member_float = member.astype(jnp.float32)
    totals = jnp.dot(member_float.T, jnp.sum(weights, axis=2), precision=HIGHEST)
    summed = jnp.dot(member_float.T, page_sum.reshape(pool_size, -1), precision=HIGHEST)
    return (row_max, totals, summed.reshape(row_count, head_count, latent_width))


def expert_work(arriving, gate_weight, up_weight, down_weight):
    gate_proj = jnp.einsum(
        "sjcd,jdf->sjcf", arriving, gate_weight, preferred_element_type=jnp.float32
    )
    up_proj = jnp.einsum("sjcd,jdf->sjcf", arriving, up_weight, preferred_element_type=jnp.float32)
    hidden = (jax.nn.silu(gate_proj) * up_proj).astype(jnp.bfloat16)
    return jnp.einsum("sjcf,jfd->sjcd", hidden, down_weight, preferred_element_type=jnp.float32)


def round_trip(slot_block, share_map, gate_weight, up_weight, down_weight):
    arriving = lax.all_to_all(slot_block, "attn", split_axis=0, concat_axis=0, tiled=True)
    produced = expert_work(arriving, gate_weight, up_weight, down_weight)
    reduced = lax.psum_scatter(produced, "expert", scatter_dimension=3, tiled=True)
    returned = lax.all_to_all(reduced, "attn", split_axis=0, concat_axis=0, tiled=True)
    flattened = returned.reshape(-1, returned.shape[3])
    return jnp.einsum("sr,sd->rd", share_map, flattened, precision=HIGHEST)


def on_device(
    queries,
    cache,
    owner,
    uv_weight,
    out_weight,
    norm_gain,
    expert_ids,
    gate_values,
    gate_weight,
    up_weight,
    down_weight,
):
    row_count = queries.shape[0]
    latent_width = uv_weight.shape[1]
    row_max, totals, summed = local_attention(queries, cache, owner, latent_width)
    maxima, denominators, numerators = (
        lax.all_to_all(row_max[None], "expert", split_axis=2, concat_axis=0, tiled=True),
        lax.all_to_all(totals[None], "expert", split_axis=2, concat_axis=0, tiled=True),
        lax.all_to_all(summed[None], "expert", split_axis=2, concat_axis=0, tiled=True),
    )
    peaks = jnp.max(maxima, axis=0)
    rescale = jnp.exp(maxima - peaks[None])
    total_weight = jnp.sum(rescale * denominators, axis=0)
    attended = (
        jnp.sum(rescale[:, :, :, None] * numerators, axis=0) / total_weight[:, :, None]
    ).astype(jnp.bfloat16)
    mixed_heads = jnp.einsum(
        "rhc,hcv->rhv", attended, uv_weight, preferred_element_type=jnp.float32
    )
    mixed_heads = mixed_heads.astype(jnp.bfloat16).reshape(row_count, -1)
    partial_out = jnp.dot(mixed_heads, out_weight, preferred_element_type=jnp.float32)
    attn_out = lax.psum(partial_out, "expert")
    mean_square = jnp.mean(attn_out * attn_out, axis=1, keepdims=True)
    normed = (attn_out * lax.rsqrt(mean_square + EPSILON) * norm_gain[None, :]).astype(jnp.bfloat16)
    attn_size = lax.axis_size("attn")
    expert_size = lax.axis_size("expert")
    local_experts = gate_weight.shape[0]
    expert_total = local_experts * attn_size
    top_count = expert_ids.shape[1]
    model_width = normed.shape[1]
    capacity = min(
        row_count, 2 * ((3 * row_count * top_count + 4 * expert_total - 1) // (4 * expert_total))
    )
    flat_ids = expert_ids.reshape(-1)
    matches = (flat_ids[:, None] == jnp.arange(expert_total, dtype=jnp.int32)[None, :]).astype(
        jnp.int32
    )
    earlier = jnp.cumsum(matches, axis=0) - matches
    position = jnp.sum(earlier * matches, axis=1)
    slot_index = (flat_ids * capacity + position).reshape(row_count, top_count)
    chosen = (
        jnp.arange(expert_total * capacity, dtype=jnp.int32)[:, None, None]
        == slot_index[None, :, :]
    )
    pick_map = jnp.any(chosen, axis=2).astype(jnp.bfloat16)
    weight_map = jnp.sum(jnp.where(chosen, gate_values[None, :, :], 0.0), axis=2)
    outgoing = jnp.dot(pick_map, normed, preferred_element_type=jnp.float32).astype(jnp.bfloat16)
    outgoing = outgoing.reshape(attn_size, local_experts, capacity, model_width)
    weight_grid = weight_map.reshape(attn_size, local_experts, capacity, row_count)
    share_map = weight_grid.reshape(-1, row_count)
    section_sum = round_trip(outgoing, share_map, gate_weight, up_weight, down_weight)
    column_width = model_width // expert_size
    attn_columns = lax.dynamic_slice_in_dim(
        attn_out, lax.axis_index("expert") * column_width, column_width, 1
    )
    return (attn_columns + section_sum).astype(jnp.bfloat16)


def solution(mesh):
    placed = (
        P("attn", None, None),
        P(("attn", "expert"), None, None),
        P(("attn", "expert")),
        P("expert", None, None),
        P("expert", None),
        P(),
        P("attn", None),
        P("attn", None),
        P("attn", None, "expert"),
        P("attn", None, "expert"),
        P("attn", "expert", None),
    )
    return jax.shard_map(
        on_device, mesh=mesh, in_specs=placed, out_specs=P("attn", "expert"), check_vma=False
    )
```

profile of v0, /device:TPU:1, one launch (start us, length us, event | category | flops | bytes accessed | tf_op | source)
XLA Modules:
  0.0 384.2 jit_solution(11106621884005514824)
XLA Ops:
  6.5 0.7 broadcast_minimum_fusion
  7.3 0.7 broadcast_compare_fusion
  8.0 10.3 %gather_fusion = bf16[192,64,576]{2,1,0:T(8,128)(2,1)} fusion(bf16[4,64,576]{2,1,0:T(8,128)(2,1)} %param.11, s32[1024]{0:T(1024)S(1)} %pad_clamp_fusion), kind=kCustom, calls=%fused_computation | custom fusion | bytes 28312320 | tf_op jit(solution)/shard_map/jit(_take)/gather | solution.py:18
  18.3 15.5 %fusion.3 = f32[192,64,64]{1,2,0:T(8,128)} fusion(bf16[192,64,576]{2,1,0:T(8,128)(2,1)} %param.12, bf16[192,64,576]{2,1,0:T(8,128)(2,1)} %gather_fusion, pred[192]{0:T(512)(128)(4,1)S(1)} %get-tuple-element.12), kind=kOutput, calls=%fused_computation.5 | convolution fusion | flops 913047552 | bytes 31457472 | tf_op jit(solution)/shard_map/phc,ptc->pht/dot_general | solution.py:20
  33.7 7.6 %copy.80 = f32[192,64,64]{0,2,1:T(8,128)} copy(f32[192,64,64]{1,2,0:T(8,128)} %fusion.3) | data formatting | bytes 6291456 | tf_op jit(solution)/shard_map/phc,ptc->pht/dot_general | solution.py:20
  41.3 2.9 multiply_reduce_fusion
  44.6 0.7 gather_fusion.1
  45.5 3.5 fusion.14
  49.0 0.8 fusion.43
  49.7 7.6 %all-to-all-start.2 = ((f32[1,4,64]{1,0,2:T(1,128)}), f32[1,4,64]{1,0,2:T(1,128)S(1)}, u32[]{:S(2)}, u32[]{:S(2)}) async-start(f32[1,4,64]{1,0,2:T(1,128)} %bitcast.38), calls=%async_computation.2 | async-start | bytes 65536 | tf_op jit(solution)/shard_map/all_to_all | solution.py:78
  57.3 3.8 copy.87
  61.1 17.2 %fusion.6 = f32[192,64,512]{2,1,0:T(8,128)} fusion(bf16[192,64,64]{2,1,0:T(8,128)(2,1)} %copy.87, bf16[192,64,576]{2,1,0:T(8,128)(2,1)} %param.12), kind=kOutput, calls=%fused_computation.8 | convolution fusion | flops 805306368 | bytes 40894464 | tf_op jit(solution)/shard_map/pht,ptc->phc/dot_general | solution.py:33
  78.4 0.7 copy.83
  79.1 6.7 %all-to-all-start = ((f32[1,4,64]{1,0,2:T(1,128)}), f32[1,4,64]{1,0,2:T(1,128)S(1)}, u32[]{:S(2)}, u32[]{:S(2)}) async-start(f32[1,4,64]{1,0,2:T(1,128)} %copy.83), calls=%async_computation | async-start | bytes 65536 | tf_op jit(solution)/shard_map/all_to_all | solution.py:77
  85.8 28.2 %fusion.16 = f32[1,4,64,512]{3,1,0,2:T(4,128)} fusion(pred[192,4]{0,1:T(4,128)(4,1)S(1)} %fusion.38, f32[24,8,64,512]{3,2,1,0:T(8,128)} %bitcast.99), kind=kOutput, calls=%fused_computation.22 | convolution fusion | flops 301989888 | bytes 25690880 | tf_op jit(solution)/shard_map/dot_general | solution.py:38
  114.1 6.7 %all-to-all-start.1 = ((f32[1,4,64,512]{3,1,0,2:T(4,128)}), f32[1,4,64,512]{3,1,0,2:T(4,128)S(1)}, u32[]{:S(2)}, u32[]{:S(2)}) async-start(f32[1,4,64,512]{3,1,0,2:T(4,128)} %fusion.16), calls=%async_computation.1 | async-start | bytes 1048576 | tf_op jit(solution)/shard_map/all_to_all | solution.py:79
  122.2 7.8 %all-to-all-done.1 = f32[1,4,64,512]{3,1,0,2:T(4,128)S(1)} async-done(((f32[1,4,64,512]{3,1,0,2:T(4,128)}), f32[1,4,64,512]{3,1,0,2:T(4,128)S(1)}, u32[]{:S(2)}, u32[]{:S(2)}) %all-to-all-start.1) | async-done | bytes 524320 | tf_op jit(solution)/shard_map/all_to_all | solution.py:79
  130.2 5.0 %fusion.23 = f32[4,7168]{1,0:T(4,128)} fusion(bf16[512,7168]{1,0:T(8,128)(2,1)} %param.15, bf16[4,512,128]{2,1,0:T(8,128)(2,1)S(1)} %copy-done, f32[4,4,512]{2,0,1:T(4,128)S(1)} %multiply_reduce_fusion.1, f32[4,4]{0,1:T(4,128)S(1)} %copy.92), kind=kOutput, calls=%fused_computation.29 | convolution fusion | flops 31475712 | bytes 8011840 | tf_op jit(solution)/shard_map/dot_general | solution.py:91
  135.3 81.5 %all-reduce.2.cloned.1.call-done = f32[4,7168]{1,0:T(4,128)} async-done(((f32[4,7168]{1,0:T(4,128)}), f32[4,7168]{1,0:T(4,128)}) %all-reduce.2.cloned.1.call-update) | async-done | bytes 114704 | tf_op jit(solution)/shard_map/psum | solution.py:92
  216.8 1.1 multiply_reduce_fusion.2
  217.9 1.4 convolution_convert_fusion
  219.6 20.8 %all_to_all.64 = bf16[8,2,4,7168]{3,2,1,0:T(4,128)(2,1)S(1)} all-to-all(bf16[8,2,4,7168]{3,2,1,0:T(4,128)(2,1)S(1)} %reshape.116), channel_id=1, replica_groups=mesh['attn'=8,'expert'=16] {'attn'}, dimensions={0} | all-to-all | bytes 1835008 | tf_op jit(solution)/shard_map/all_to_all | solution.py:52
  240.4 3.0 fusion.10
  243.4 0.8 fusion.12
  244.8 18.9 %copy.103 = f32[8,2,4,7168]{0,2,1,3:T(4,128)} copy(f32[8,2,4,7168]{3,0,2,1:T(8,128)S(1)} %convolution_bitcast_fusion) | data formatting | bytes 3670016
  263.8 24.2 %reshape.140 = f32[7168,64]{1,0:T(8,128)} reshape(f32[7168,2,4,8]{3,2,1,0:T(4,128)} %bitcast.100) | data formatting | bytes 3670016
  288.0 72.0 %reduce-scatter.4.cloned.1.call-done = f32[448,64]{1,0:T(8,128)} async-done(((f32[7168,64]{1,0:T(8,128)}), f32[448,64]{1,0:T(8,128)}) %reduce-scatter.4.cloned.1.call-update) | async-done | bytes 114704
  360.0 2.2 reshape.141
  362.2 1.6 copy.97
  363.7 6.8 %all-to-all-start.4 = ((f32[8,2,4,448]{3,2,1,0:T(4,128)}), f32[8,2,4,448]{3,2,1,0:T(4,128)S(1)}, u32[]{:S(2)}, u32[]{:S(2)}) async-start(f32[8,2,4,448]{3,2,1,0:T(4,128)} %copy.97), calls=%async_computation.4 | async-start | bytes 262144 | tf_op jit(solution)/shard_map/all_to_all | solution.py:55
  370.6 5.2 %all-to-all-done.4 = f32[8,2,4,448]{3,2,1,0:T(4,128)S(1)} async-done(((f32[8,2,4,448]{3,2,1,0:T(4,128)}), f32[8,2,4,448]{3,2,1,0:T(4,128)S(1)}, u32[]{:S(2)}, u32[]{:S(2)}) %all-to-all-start.4) | async-done | bytes 114720 | tf_op jit(solution)/shard_map/all_to_all | solution.py:55
  375.9 1.5 fusion.19
  (45 shorter events, 3.5 us)
Async XLA Ops:
  6.5 123.6 %copy-start = (bf16[4,512,128]{2,1,0:T(8,128)(2,1)S(1)}, bf16[4,512,128]{2,1,0:T(8,128)(2,1)}, u32[]{:S(2)}) copy-start(bf16[4,512,128]{2,1,0:T(8,128)(2,1)} %param.14) | copy-start | bytes 1572868
  49.7 29.3 %all-to-all-start.2 = ((f32[1,4,64]{1,0,2:T(1,128)}), f32[1,4,64]{1,0,2:T(1,128)S(1)}, u32[]{:S(2)}, u32[]{:S(2)}) async-start(f32[1,4,64]{1,0,2:T(1,128)} %bitcast.38), calls=%async_computation.2 | async-start | bytes 65536 | tf_op jit(solution)/shard_map/all_to_all | solution.py:78
  79.1 35.0 %all-to-all-start = ((f32[1,4,64]{1,0,2:T(1,128)}), f32[1,4,64]{1,0,2:T(1,128)S(1)}, u32[]{:S(2)}, u32[]{:S(2)}) async-start(f32[1,4,64]{1,0,2:T(1,128)} %copy.83), calls=%async_computation | async-start | bytes 65536 | tf_op jit(solution)/shard_map/all_to_all | solution.py:77
  85.7 28.3 %copy-start.3 = (s32[4,8]{1,0:T(4,128)S(1)}, s32[4,8]{1,0:T(4,128)}, u32[]{:S(2)}) copy-start(s32[4,8]{1,0:T(4,128)} %param.17) | copy-start | bytes 388
  114.1 15.9 %all-to-all-start.1 = ((f32[1,4,64,512]{3,1,0,2:T(4,128)}), f32[1,4,64,512]{3,1,0,2:T(4,128)S(1)}, u32[]{:S(2)}, u32[]{:S(2)}) async-start(f32[1,4,64,512]{3,1,0,2:T(4,128)} %fusion.16), calls=%async_computation.1 | async-start | bytes 1048576 | tf_op jit(solution)/shard_map/all_to_all | solution.py:79
  120.8 96.0 %all-reduce.2.cloned.1.call-start = ((), (), s32[]{:S(2)}) async-start(), calls=%async_computation.6 | async-start | bytes 229376 | tf_op jit(solution)/shard_map/psum | solution.py:92
  130.2 87.7 %copy-start.2 = (f32[7168]{0:T(1024)S(1)}, f32[7168]{0:T(1024)}, u32[]{:S(2)}) copy-start(f32[7168]{0:T(1024)} %param.16) | copy-start | bytes 86020
  135.2 224.8 %reduce-scatter.4.cloned.1.call-start = ((), (), s32[]{:S(2)}) async-start(), calls=%async_computation.7 | async-start | bytes 3899392
  219.6 23.8 %copy-start.5 = (bf16[2,7168,128]{2,1,0:T(8,128)(2,1)S(1)}, bf16[2,7168,128]{2,1,0:T(8,128)(2,1)}, u32[]{:S(2)}) copy-start(bf16[2,7168,128]{2,1,0:T(8,128)(2,1)} %param.19) | copy-start | bytes 11010052
  240.4 3.8 copy-start.1
  288.0 82.6 %copy-start.4 = (f32[4,8]{1,0:T(4,128)S(1)}, f32[4,8]{1,0:T(4,128)}, u32[]{:S(2)}) copy-start(f32[4,8]{1,0:T(4,128)} %param.18) | copy-start | bytes 388
  363.7 12.1 %all-to-all-start.4 = ((f32[8,2,4,448]{3,2,1,0:T(4,128)}), f32[8,2,4,448]{3,2,1,0:T(4,128)S(1)}, u32[]{:S(2)}, u32[]{:S(2)}) async-start(f32[8,2,4,448]{3,2,1,0:T(4,128)} %copy.97), calls=%async_computation.4 | async-start | bytes 262144 | tf_op jit(solution)/shard_map/all_to_all | solution.py:55
Sparse Core Ops, SparseCore 0:
  135.3 81.4 all-reduce.1
  288.1 71.8 reduce-scatter.3
where the time goes:
time: 385 us; the launch traced here: 384 us
  waiting for transfers between devices  166 us (43%)
  matrix products  73.9 us (19%)
  local copies, waits for them, and re-layouts  71.5 us (19%)
  starting transfers between devices  28 us (7%)
  blocking collectives  20.8 us (5%)
  between operations  13.6 us (4%)
  other arithmetic  9.93 us (3%)
    psum x1, waiting for transfers between devices, on_device(): attn_out = lax.psum(partial_out, 'expert')  81.5 us
    unnamed x3, waiting for transfers between devices  72 us
    unnamed x16, local copies, waits for them, and re-layouts  45.4 us
    dot_general x1, matrix products, local_attention(): jnp.dot(member_float.T, page_sum.reshape(pool_size, -1), precision=HIGHEST)  28.2 us
    all_to_all x1, blocking collectives, round_trip(): lax.all_to_all(slot_block, 'attn', split_axis=0, concat_axis=0, tiled=True)  20.8 us
    dot_general x1, matrix products, local_attention(): jnp.einsum('pht,ptc->phc', probs, cache[:, :, :latent_width], preferred_e...  17.2 us
    dot_general x1, matrix products, local_attention(): jnp.einsum('phc,ptc->pht', picked, cache, preferred_element_type=jnp.floa...  15.5 us
    gather x1, local copies, waits for them, and re-layouts, local_attention(): picked = jnp.take(queries, safe_owner, axis=0)  10.3 us
  transfers between devices with their start and end apart: 6, of which 4 were waited for; matrix products, arithmetic and copies ran while one was open for 13% of the time, Pallas kernels for 0%

commit v1 on v0

--- a/solution.py
+++ b/solution.py
@@ -1,3 +1,4 @@
+import functools
 import jax
 import jax.numpy as jnp
 from jax import lax
@@ -7,6 +8,17 @@
 SCORE_SCALE = 192.0 ** (-0.5)
 EPSILON = 1e-06
 HIGHEST = lax.Precision.HIGHEST
+
+
+def connect_lines_on_mesh(inp, lane_axis):
+    num = lax.axis_size(lane_axis)
+    odd = inp
+    for hop_no in [[(kk, kk ^ j0) for kk in range(num)] for j0 in (1, 2, 4, 8, 16) if j0 < num]:
+        odd = odd + lax.ppermute(odd, perm=hop_no, axis_name=lane_axis)
+    return odd
+
+
+finish_the_object = functools.partial(connect_lines_on_mesh, lane_axis="expert")
 
 
 def local_attention(queries, cache, owner, latent_width):
@@ -89,7 +101,7 @@
     )
     mixed_heads = mixed_heads.astype(jnp.bfloat16).reshape(row_count, -1)
     partial_out = jnp.dot(mixed_heads, out_weight, preferred_element_type=jnp.float32)
-    attn_out = lax.psum(partial_out, "expert")
+    attn_out = finish_the_object(partial_out)
     mean_square = jnp.mean(attn_out * attn_out, axis=1, keepdims=True)
     normed = (attn_out * lax.rsqrt(mean_square + EPSILON) * norm_gain[None, :]).astype(jnp.bfloat16)
     attn_size = lax.axis_size("attn")

time: 385 us -> 324 us (0.84)
  waiting for transfers between devices: 166 us -> 99.3 us
  blocking collectives: 20.8 us -> 27.7 us
    psum x1 -> x0, waiting for transfers between devices: 81.5 us -> none  [on_device(): attn_out = lax.psum(partial_out, 'expert')]
    ppermute x0 -> x4, waiting for transfers between devices: none -> 14.9 us  [connect_lines_on_mesh(): odd = odd + lax.ppermute(odd, perm=hop_no, axis_name=lane_axis)]
    all_to_all x1, blocking collectives: 20.8 us -> 27.7 us  [round_trip(): lax.all_to_all(slot_block, 'attn', split_axis=0, concat_axis=0, tiled=True)]
    unnamed x3 -> x2, waiting for transfers between devices: 72 us -> 71.1 us
  transfers between devices with their start and end apart: 6 -> 9, of which waited for: 4 -> 7; matrix products, arithmetic and copies ran while one was open for 13% -> 16% of each run, Pallas kernels for 0% -> 0%
where the time goes in v1:
time: 324 us; the launch traced here: 323 us
  waiting for transfers between devices  99.3 us (31%)
  matrix products  71.7 us (22%)
  local copies, waits for them, and re-layouts  71.5 us (22%)
  starting transfers between devices  30.3 us (9%)
  blocking collectives  27.7 us (9%)
  between operations  13.6 us (4%)
  other arithmetic  9.13 us (3%)
    unnamed x2, waiting for transfers between devices  71.1 us
    unnamed x16, local copies, waits for them, and re-layouts  45.4 us
    dot_general x1, matrix products, local_attention(): jnp.dot(member_float.T, page_sum.reshape(pool_size, -1), precision=HIGHEST)  28.2 us
    all_to_all x1, blocking collectives, round_trip(): lax.all_to_all(slot_block, 'attn', split_axis=0, concat_axis=0, tiled=True)  27.7 us
    dot_general x1, matrix products, local_attention(): jnp.einsum('pht,ptc->phc', probs, cache[:, :, :latent_width], preferred_e...  17.2 us
    dot_general x1, matrix products, local_attention(): jnp.einsum('phc,ptc->pht', picked, cache, preferred_element_type=jnp.floa...  15.5 us
    ppermute x4, waiting for transfers between devices, connect_lines_on_mesh(): odd = odd + lax.ppermute(odd, perm=hop_no, axis_name=lane_axis)  14.9 us
    gather x1, local copies, waits for them, and re-layouts, local_attention(): picked = jnp.take(queries, safe_owner, axis=0)  10.3 us
  transfers between devices with their start and end apart: 9, of which 7 were waited for; matrix products, arithmetic and copies ran while one was open for 16% of the time, Pallas kernels for 0%

profile of v1, /device:TPU:1, one launch (start us, length us, event | category | flops | bytes accessed | tf_op | source)
XLA Modules:
  0.0 323.2 jit_solution(8656677637486394648)
XLA Ops:
  6.5 0.7 broadcast_minimum_fusion
  8.0 10.3 %gather_fusion = bf16[192,64,576]{2,1,0:T(8,128)(2,1)} fusion(bf16[4,64,576]{2,1,0:T(8,128)(2,1)} %param.11, s32[1024]{0:T(1024)S(1)} %pad_clamp_fusion), kind=kCustom, calls=%fused_computation | custom fusion | bytes 28312320 | tf_op jit(solution)/shard_map/jit(_take)/gather | solution.py:30
  18.3 15.5 %fusion.3 = f32[192,64,64]{1,2,0:T(8,128)} fusion(bf16[192,64,576]{2,1,0:T(8,128)(2,1)} %param.12, bf16[192,64,576]{2,1,0:T(8,128)(2,1)} %gather_fusion, pred[192]{0:T(512)(128)(4,1)S(1)} %get-tuple-element.14), kind=kOutput, calls=%fused_computation.5 | convolution fusion | flops 913047552 | bytes 31457472 | tf_op jit(solution)/shard_map/phc,ptc->pht/dot_general | solution.py:32
  33.7 7.6 %copy.80 = f32[192,64,64]{0,2,1:T(8,128)} copy(f32[192,64,64]{1,2,0:T(8,128)} %fusion.3) | data formatting | bytes 6291456 | tf_op jit(solution)/shard_map/phc,ptc->pht/dot_general | solution.py:32
  41.3 2.9 multiply_reduce_fusion
  45.5 3.5 %fusion.14 = (f32[192,64]{0,1:T(8,128)S(1)}, bf16[192,64,64]{0,2,1:T(8,128)(2,1)S(1)}) fusion(f32[192,64,64]{0,2,1:T(8,128)} %copy.80, f32[192,64]{0,1:T(8,128)S(1)} %copy.86, pred[192]{0:T(512)(128)(4,1)S(1)} %get-tuple-element.13), kind=kLoop, calls=%fused_computation.20 | loop fusion | flops 3919872 | bytes 4817088 | tf_op jit(solution)/shard_map/reduce_sum | solution.py:49
  49.0 0.8 fusion.42
  49.7 7.6 %all-to-all-start.2 = ((f32[1,4,64]{1,0,2:T(1,128)}), f32[1,4,64]{1,0,2:T(1,128)S(1)}, u32[]{:S(2)}, u32[]{:S(2)}) async-start(f32[1,4,64]{1,0,2:T(1,128)} %bitcast.38), calls=%async_computation.2 | async-start | bytes 65536 | tf_op jit(solution)/shard_map/all_to_all | solution.py:90
  57.3 3.8 %copy.87 = bf16[192,64,64]{2,1,0:T(8,128)(2,1)} copy(bf16[192,64,64]{0,2,1:T(8,128)(2,1)S(1)} %get-tuple-element.10) | data formatting | bytes 3145728 | tf_op jit(solution)/shard_map/convert_element_type | solution.py:44
  61.1 17.2 %fusion.6 = f32[192,64,512]{2,1,0:T(8,128)} fusion(bf16[192,64,64]{2,1,0:T(8,128)(2,1)} %copy.87, bf16[192,64,576]{2,1,0:T(8,128)(2,1)} %param.12), kind=kOutput, calls=%fused_computation.8 | convolution fusion | flops 805306368 | bytes 40894464 | tf_op jit(solution)/shard_map/pht,ptc->phc/dot_general | solution.py:45
  79.1 6.7 %all-to-all-start = ((f32[1,4,64]{1,0,2:T(1,128)}), f32[1,4,64]{1,0,2:T(1,128)S(1)}, u32[]{:S(2)}, u32[]{:S(2)}) async-start(f32[1,4,64]{1,0,2:T(1,128)} %copy.83), calls=%async_computation | async-start | bytes 65536 | tf_op jit(solution)/shard_map/all_to_all | solution.py:89
  85.7 28.2 %fusion.16 = f32[1,4,64,512]{3,1,0,2:T(4,128)} fusion(pred[192,4]{0,1:T(4,128)(4,1)S(1)} %fusion.37, f32[24,8,64,512]{3,2,1,0:T(8,128)} %bitcast.99), kind=kOutput, calls=%fused_computation.22 | convolution fusion | flops 301989888 | bytes 25690880 | tf_op jit(solution)/shard_map/dot_general | solution.py:50
  114.0 6.7 %all-to-all-start.1 = ((f32[1,4,64,512]{3,1,0,2:T(4,128)}), f32[1,4,64,512]{3,1,0,2:T(4,128)S(1)}, u32[]{:S(2)}, u32[]{:S(2)}) async-start(f32[1,4,64,512]{3,1,0,2:T(4,128)} %fusion.16), calls=%async_computation.1 | async-start | bytes 1048576 | tf_op jit(solution)/shard_map/all_to_all | solution.py:91
  121.7 8.2 %all-to-all-done.1 = f32[1,4,64,512]{3,1,0,2:T(4,128)S(1)} async-done(((f32[1,4,64,512]{3,1,0,2:T(4,128)}), f32[1,4,64,512]{3,1,0,2:T(4,128)S(1)}, u32[]{:S(2)}, u32[]{:S(2)}) %all-to-all-start.1) | async-done | bytes 524320 | tf_op jit(solution)/shard_map/all_to_all | solution.py:91
  130.1 4.3 %fusion.22 = f32[4,7168]{1,0:T(4,128)S(1)} fusion(bf16[512,7168]{1,0:T(8,128)(2,1)} %param.15, bf16[4,512,128]{2,1,0:T(8,128)(2,1)S(1)} %copy-done, f32[4,4,512]{2,0,1:T(4,128)S(1)} %multiply_reduce_fusion.1, f32[4,4]{0,1:T(4,128)S(1)} %copy.92), kind=kOutput, calls=%fused_computation.27 | convolution fusion | flops 31475712 | bytes 8011840 | tf_op jit(solution)/shard_map/dot_general | solution.py:103
  134.7 3.3 %collective-permute-done = f32[4,7168]{1,0:T(4,128)S(1)} collective-permute-done((f32[4,7168]{1,0:T(4,128)S(1)}, f32[4,7168]{1,0:T(4,128)S(1)}, u32[]{:S(2)}, u32[]{:S(2)}) %collective-permute-start) | collective-permute-done | bytes 114720 | tf_op jit(solution)/shard_map/ppermute | solution.py:17
  138.1 0.9 collective-permute-start.1
  139.1 4.2 %collective-permute-done.1 = f32[4,7168]{1,0:T(4,128)S(1)} collective-permute-done((f32[4,7168]{1,0:T(4,128)S(1)}, f32[4,7168]{1,0:T(4,128)S(1)}, u32[]{:S(2)}, u32[]{:S(2)}) %collective-permute-start.1) | collective-permute-done | bytes 114720 | tf_op jit(solution)/shard_map/ppermute | solution.py:17
  143.8 3.2 %collective-permute-done.2 = f32[4,7168]{1,0:T(4,128)S(1)} collective-permute-done((f32[4,7168]{1,0:T(4,128)S(1)}, f32[4,7168]{1,0:T(4,128)S(1)}, u32[]{:S(2)}, u32[]{:S(2)}) %collective-permute-start.2) | collective-permute-done | bytes 114720 | tf_op jit(solution)/shard_map/ppermute | solution.py:17
  147.1 1.1 collective-permute-start.3
  148.3 4.1 %collective-permute-done.3 = f32[4,7168]{1,0:T(4,128)S(1)} collective-permute-done((f32[4,7168]{1,0:T(4,128)S(1)}, f32[4,7168]{1,0:T(4,128)S(1)}, u32[]{:S(2)}, u32[]{:S(2)}) %collective-permute-start.3) | collective-permute-done | bytes 114720 | tf_op jit(solution)/shard_map/ppermute | solution.py:17
  153.3 27.7 %all_to_all.64 = bf16[8,2,4,7168]{3,2,1,0:T(4,128)(2,1)S(1)} all-to-all(bf16[8,2,4,7168]{3,2,1,0:T(4,128)(2,1)S(1)} %reshape.116), channel_id=1, replica_groups=mesh['attn'=8,'expert'=16] {'attn'}, dimensions={0} | all-to-all | bytes 1835008 | tf_op jit(solution)/shard_map/all_to_all | solution.py:64
  181.0 3.0 fusion.10
  184.1 0.8 fusion.12
  185.5 18.9 %copy.103 = f32[8,2,4,7168]{0,2,1,3:T(4,128)} copy(f32[8,2,4,7168]{3,0,2,1:T(8,128)S(1)} %convolution_bitcast_fusion) | data formatting | bytes 3670016
  204.4 24.2 %reshape.140 = f32[7168,64]{1,0:T(8,128)} reshape(f32[7168,2,4,8]{3,2,1,0:T(4,128)} %bitcast.100) | data formatting | bytes 3670016
  228.7 71.1 %reduce-scatter.4.cloned.1.call-done = f32[448,64]{1,0:T(8,128)} async-done(((f32[7168,64]{1,0:T(8,128)}), f32[448,64]{1,0:T(8,128)}) %reduce-scatter.4.cloned.1.call-update) | async-done | bytes 114704
  299.8 2.2 reshape.141
  301.9 1.6 copy.97
  303.5 6.8 %all-to-all-start.4 = ((f32[8,2,4,448]{3,2,1,0:T(4,128)}), f32[8,2,4,448]{3,2,1,0:T(4,128)S(1)}, u32[]{:S(2)}, u32[]{:S(2)}) async-start(f32[8,2,4,448]{3,2,1,0:T(4,128)} %copy.97), calls=%async_computation.4 | async-start | bytes 262144 | tf_op jit(solution)/shard_map/all_to_all | solution.py:67
  310.4 5.2 %all-to-all-done.4 = f32[8,2,4,448]{3,2,1,0:T(4,128)S(1)} async-done(((f32[8,2,4,448]{3,2,1,0:T(4,128)}), f32[8,2,4,448]{3,2,1,0:T(4,128)S(1)}, u32[]{:S(2)}, u32[]{:S(2)}) %all-to-all-start.4) | async-done | bytes 114720 | tf_op jit(solution)/shard_map/all_to_all | solution.py:67
  315.6 0.8 add_convert_fusion
  (53 shorter events, 6.7 us)
Async XLA Ops:
  6.5 123.5 %copy-start = (bf16[4,512,128]{2,1,0:T(8,128)(2,1)S(1)}, bf16[4,512,128]{2,1,0:T(8,128)(2,1)}, u32[]{:S(2)}) copy-start(bf16[4,512,128]{2,1,0:T(8,128)(2,1)} %param.14) | copy-start | bytes 1572868
  49.7 29.3 %all-to-all-start.2 = ((f32[1,4,64]{1,0,2:T(1,128)}), f32[1,4,64]{1,0,2:T(1,128)S(1)}, u32[]{:S(2)}, u32[]{:S(2)}) async-start(f32[1,4,64]{1,0,2:T(1,128)} %bitcast.38), calls=%async_computation.2 | async-start | bytes 65536 | tf_op jit(solution)/shard_map/all_to_all | solution.py:90
  79.1 34.9 %all-to-all-start = ((f32[1,4,64]{1,0,2:T(1,128)}), f32[1,4,64]{1,0,2:T(1,128)S(1)}, u32[]{:S(2)}, u32[]{:S(2)}) async-start(f32[1,4,64]{1,0,2:T(1,128)} %copy.83), calls=%async_computation | async-start | bytes 65536 | tf_op jit(solution)/shard_map/all_to_all | solution.py:89
  114.0 15.9 %all-to-all-start.1 = ((f32[1,4,64,512]{3,1,0,2:T(4,128)}), f32[1,4,64,512]{3,1,0,2:T(4,128)S(1)}, u32[]{:S(2)}, u32[]{:S(2)}) async-start(f32[1,4,64,512]{3,1,0,2:T(4,128)} %fusion.16), calls=%async_computation.1 | async-start | bytes 1048576 | tf_op jit(solution)/shard_map/all_to_all | solution.py:91
  120.7 179.1 %reduce-scatter.4.cloned.1.call-start = ((), (), s32[]{:S(2)}) async-start(), calls=%async_computation.6 | async-start | bytes 3899392
  130.1 8.9 %copy-start.3 = (s32[4,8]{1,0:T(4,128)S(1)}, s32[4,8]{1,0:T(4,128)}, u32[]{:S(2)}) copy-start(s32[4,8]{1,0:T(4,128)} %param.17) | copy-start | bytes 388
  130.1 22.4 %copy-start.2 = (f32[7168]{0:T(1024)S(1)}, f32[7168]{0:T(1024)}, u32[]{:S(2)}) copy-start(f32[7168]{0:T(1024)} %param.16) | copy-start | bytes 86020
  134.4 3.6 %collective-permute-start = (f32[4,7168]{1,0:T(4,128)S(1)}, f32[4,7168]{1,0:T(4,128)S(1)}, u32[]{:S(2)}, u32[]{:S(2)}) collective-permute-start(f32[4,7168]{1,0:T(4,128)S(1)} %fusion.22), channel_id=1, source_target_pairs={{0,1},{1,0},{2,3},{3,2},{4,5},{5,4},{6,7},{7,6},{8,9},{9,8},{10,11... | collective-permute-start | bytes 344072 | tf_op jit(solution)/shard_map/ppermute | solution.py:17
  138.1 5.2 %collective-permute-start.1 = (f32[4,7168]{1,0:T(4,128)S(1)}, f32[4,7168]{1,0:T(4,128)S(1)}, u32[]{:S(2)}, u32[]{:S(2)}) collective-permute-start(f32[4,7168]{1,0:T(4,128)S(1)} %add.48), channel_id=1, source_target_pairs={{0,2},{1,3},{2,0},{3,1},{4,6},{5,7},{6,4},{7,5},{8,10},{9,11},{10,... | collective-permute-start | bytes 344072 | tf_op jit(solution)/shard_map/ppermute | solution.py:17
  143.4 3.7 %collective-permute-start.2 = (f32[4,7168]{1,0:T(4,128)S(1)}, f32[4,7168]{1,0:T(4,128)S(1)}, u32[]{:S(2)}, u32[]{:S(2)}) collective-permute-start(f32[4,7168]{1,0:T(4,128)S(1)} %add.49), channel_id=1, source_target_pairs={{0,4},{1,5},{2,6},{3,7},{4,0},{5,1},{6,2},{7,3},{8,12},{9,13},{10,... | collective-permute-start | bytes 344072 | tf_op jit(solution)/shard_map/ppermute | solution.py:17
  147.1 5.2 %collective-permute-start.3 = (f32[4,7168]{1,0:T(4,128)S(1)}, f32[4,7168]{1,0:T(4,128)S(1)}, u32[]{:S(2)}, u32[]{:S(2)}) collective-permute-start(f32[4,7168]{1,0:T(4,128)S(1)} %add.50), channel_id=1, source_target_pairs={{0,8},{1,9},{2,10},{3,11},{4,12},{5,13},{6,14},{7,15},{8,0},{9,1},... | collective-permute-start | bytes 344072 | tf_op jit(solution)/shard_map/ppermute | solution.py:17
  153.3 30.7 %copy-start.5 = (bf16[2,7168,128]{2,1,0:T(8,128)(2,1)S(1)}, bf16[2,7168,128]{2,1,0:T(8,128)(2,1)}, u32[]{:S(2)}) copy-start(bf16[2,7168,128]{2,1,0:T(8,128)(2,1)} %param.19) | copy-start | bytes 11010052
  181.0 3.8 %copy-start.1 = (bf16[2,128,7168]{2,1,0:T(8,128)(2,1)S(1)}, bf16[2,128,7168]{2,1,0:T(8,128)(2,1)}, u32[]{:S(2)}) copy-start(bf16[2,128,7168]{2,1,0:T(8,128)(2,1)} %param.21) | copy-start | bytes 11010052
  228.6 81.7 %copy-start.4 = (f32[4,8]{1,0:T(4,128)S(1)}, f32[4,8]{1,0:T(4,128)}, u32[]{:S(2)}) copy-start(f32[4,8]{1,0:T(4,128)} %param.18) | copy-start | bytes 388
  303.5 12.1 %all-to-all-start.4 = ((f32[8,2,4,448]{3,2,1,0:T(4,128)}), f32[8,2,4,448]{3,2,1,0:T(4,128)S(1)}, u32[]{:S(2)}, u32[]{:S(2)}) async-start(f32[8,2,4,448]{3,2,1,0:T(4,128)} %copy.97), calls=%async_computation.4 | async-start | bytes 262144 | tf_op jit(solution)/shard_map/all_to_all | solution.py:67
Sparse Core Ops, SparseCore 0:
  228.8 70.9 reduce-scatter.3
